TPU v7x, 128 devices: a whole 4x4x4 slice. The times are simulated.
128 devices in a mesh: scen: 4 (over y_lo, core), cell: 32 (over z, x, y_hi).
Axes of the slice: x: 4, y: 4 (y_hi: 2, y_lo: 2; y = y_hi * 2 + y_lo), z: 4, core: 2. Of those that a mesh axis runs over, the one named last changes fastest.
Arguments:
- yields: bfloat16 [12, 32, 30, 131072], P(None, 'scen', None, 'cell'), may hold values from -40 to 40, as said below
- model_factor: float32 [12, 128], replicated, may hold values from 0 to 0.5
- scen_factor: float32 [32, 128], P('scen'), may hold values from 0 to 0.30618623
- year_factor: float32 [30, 128], replicated, may hold values from 0 to 0.31622776
Outputs:
- cell_factor: float32 [131072, 128], P('cell')
- column_scale: float32 [128], replicated
- cell_gram: float32 [128, 128], replicated
Inputs may be any that keep to these rules, and one draw needn't show every extreme that they name: `yields`: yield anomalies; each cell has its own scale.
All inputs are finite; a program needn't handle non-finite values.
Results may differ from a plain program's by a relative error of at most 0.0057.
The roundings to bfloat16 on the way count: a program that leaves them out, or rounds other values in their place, can miss the bound.
Values sent between devices are 32-bit elements; how exact they have to be, the bound alone decides.
A program may use at most 128 MiB of HBM per device.

v0:
```python
import jax
import jax.numpy as jnp
from jax import lax
from jax.sharding import PartitionSpec as P

ridge = 0.1
epsilon = 1e-06


def scaled_cell(raw, total_cells):
    highest = lax.Precision.HIGHEST
    squares = lax.psum(jnp.sum(raw * raw, axis=0), "cell")
    column_scale = jnp.sqrt(squares / total_cells + epsilon)
    factor = raw / column_scale[None, :]
    products = jnp.dot(factor.T, factor, precision=highest)
    cell_gram = lax.psum(products, "cell") / total_cells
    return (factor, column_scale, cell_gram)


def on_device(yields, model_factor, scen_factor, year_factor):
    highest = lax.Precision.HIGHEST
    rank = model_factor.shape[1]
    local_cells = yields.shape[3]
    total_cells = local_cells * lax.axis_size("cell")
    khatri = (
        model_factor[:, None, None, :]
        * scen_factor[None, :, None, :]
        * year_factor[None, None, :, :]
    )
    khatri = khatri.astype(jnp.bfloat16).reshape(-1, rank)
    flat = yields.reshape(-1, local_cells)
    gram_model = jnp.dot(model_factor.T, model_factor, precision=highest)
    gram_year = jnp.dot(year_factor.T, year_factor, precision=highest)
    gram_scen = lax.psum(jnp.dot(scen_factor.T, scen_factor, precision=highest), "scen")
    normal = gram_model * gram_scen * gram_year + ridge * jnp.eye(rank, dtype=jnp.float32)
    lower = jnp.linalg.cholesky(normal)
    terms = lax.dot_general(
        flat, khatri, (((0,), (0,)), ((), ())), preferred_element_type=jnp.float32
    )
    mttkrp = lax.psum(terms, "scen")
    raw = jax.scipy.linalg.cho_solve((lower, True), mttkrp.T).T
    cell_factor, column_scale, cell_gram = scaled_cell(raw, total_cells)
    return (cell_factor, column_scale, cell_gram)


def solution(mesh):
    in_specs = (P(None, "scen", None, "cell"), P(), P("scen", None), P())
    out_specs = (P("cell", None), P(), P())
    return jax.shard_map(
        on_device, mesh=mesh, in_specs=in_specs, out_specs=out_specs, check_vma=False
    )
```

profile of v0, /device:TPU:0, one launch (start us, length us, event | category | flops | bytes accessed | tf_op | source)
XLA Modules:
  0.0 551.2 jit_solution(16899042360788201167)
XLA Ops:
  7.2 0.0 all-reduce.6.cloned.1.call-start
  7.2 1.7 fusion.14
  8.9 0.7 broadcast_multiply_fusion.1
  9.6 25.9 %fusion.2 = f32[4096,128]{0,1:T(8,128)} fusion(bf16[12,8,30,4096]{3,1,2,0:T(8,128)(2,1)} %param.4, f32[30,128]{1,0:T(8,128)} %param.7, f32[12,8,128]{2,1,0:T(8,128)S(1)} %broadcast_multiply_fusion.1), kind=kOutput, calls=%fused_computation.2 | convolution fusion | flops 3020636160 | bytes 25754624 | tf_op jit(solution)/shard_map/dot_general | solution.py:37
  35.5 0.0 copy-start.1
  35.5 0.0 copy-start.2
  35.5 0.0 all-reduce.6.cloned.1.call-update
  35.6 0.2 all-reduce.4.cloned.1.call-start
  35.8 61.0 %all-reduce.6.cloned.1.call-done = (f32[4096,128]{0,1:T(8,128)}, f32[128,128]{1,0:T(8,128)}) async-done(((f32[4096,128]{0,1:T(8,128)}, f32[128,128]{1,0:T(8,128)}), (f32[4096,128]{0,1:T(8,128)}, f32[128,128]{1,0:T(8,128)})) %all-reduce.6.cloned.1.call-update) | async-done | bytes 2162704 | tf_op jit(solution)/shard_map/psum | solution.py:40
  96.8 0.0 copy-done.1
  96.9 1.1 convolution_multiply_fusion.1
  98.0 0.0 copy-done.2
  98.0 0.3 fusion.5
  98.3 0.1 copy.7
  98.4 11.7 %cholesky.16 = f32[128,128]{1,0:T(8,128)S(1)} custom-call(f32[128,128]{1,0:T(8,128)S(1)} %fusion.13), custom_call_target="Cholesky" | custom-call | tf_op jit(solution)/shard_map/jit(cholesky)/cholesky | solution.py:36
  110.2 0.6 compare_reduce_fusion
  110.8 0.7 fusion.8
  111.5 9.8 %custom-call.10 = f32[1,128,128]{1,2,0:T(8,128)S(1)} custom-call(f32[1,128,128]{2,1,0:T(8,128)S(1)} %fusion.8), custom_call_target="InvertDiagBlocksLowerTriangular" | custom-call | tf_op jit(solution)/shard_map/jit(_cho_solve)/triangular_solve | solution.py:41
  121.3 3.5 fusion.11
  124.8 4.8 multiply_reduce_fusion
  129.6 96.3 %psum.30 = f32[128]{0:T(128)S(1)} all-reduce(f32[128]{0:T(128)S(1)} %get-tuple-element.5), channel_id=1, replica_groups=mesh['scen'=4,'cell'=32] {'cell'}, use_global_device_ids=true, to_apply=%region_5.6 | all-reduce | flops 128 | bytes 1024 | tf_op jit(solution)/shard_map/psum | solution.py:12
  225.9 0.0 copy-start.3
  225.9 1.7 broadcast_divide_fusion
  227.7 0.0 copy-done.3
  227.7 0.0 copy-start
  227.7 4.1 fusion.15
  231.8 0.0 copy-done
  231.8 0.0 all-reduce.4.cloned.1.call-update
  231.8 311.1 %all-reduce.4.cloned.1.call-done = f32[128,128]{1,0:T(8,128)} async-done(((f32[128,128]{1,0:T(8,128)}), f32[128,128]{1,0:T(8,128)}) %all-reduce.4.cloned.1.call-update) | async-done | bytes 65552 | tf_op jit(solution)/shard_map/psum | solution.py:16
  542.9 1.5 broadcast_multiply_fusion
  (3 shorter events, 0.1 us)
Async XLA Ops:
  7.2 89.7 %all-reduce.6.cloned.1.call-start = ((), (), s32[]{:S(2)}) async-start(), calls=%async_computation.1 | async-start | bytes 4325376 | tf_op jit(solution)/shard_map/psum | solution.py:40
  35.5 61.3 %copy-start.1 = (f32[12,128]{1,0:T(8,128)S(1)}, f32[12,128]{1,0:T(8,128)}, u32[]{:S(2)}) copy-start(f32[12,128]{1,0:T(8,128)} %param.5) | copy-start | bytes 18436
  35.5 62.4 %copy-start.2 = (f32[30,128]{1,0:T(8,128)S(1)}, f32[30,128]{1,0:T(8,128)}, u32[]{:S(2)}) copy-start(f32[30,128]{1,0:T(8,128)} %param.7) | copy-start | bytes 46084
  35.6 507.3 %all-reduce.4.cloned.1.call-start = ((), (), s32[]{:S(2)}) async-start(), calls=%async_computation | async-start | bytes 131072 | tf_op jit(solution)/shard_map/psum | solution.py:16
  225.9 1.7 copy-start.3
  227.7 4.1 copy-start
Sparse Core Ops, SparseCore 0:
  35.7 61.1 all-reduce.5
  231.9 310.9 all-reduce.3
where the time goes:
time: 552 us; the launch traced here: 551 us
  waiting for transfers between devices  372 us (67%)
  blocking collectives  96.3 us (17%)
  matrix products  41.5 us (8%)
  other arithmetic  26.8 us (5%)
  between operations  14.1 us (3%)
    psum x1, waiting for transfers between devices, scaled_cell(): cell_gram = lax.psum(products, 'cell') / total_cells  311 us
    psum x1, blocking collectives, scaled_cell(): squares = lax.psum(jnp.sum(raw * raw, axis=0), 'cell')  96.3 us
    psum x1, waiting for transfers between devices, on_device(): mttkrp = lax.psum(terms, 'scen')  61 us
    dot_general x1, matrix products, on_device(): lax.dot_general(flat, khatri, (((0,), (0,)), ((), ())), preferred_element...  25.9 us
    another operation x3, other arithmetic, on_device(): lower = jnp.linalg.cholesky(normal)  12.4 us
  transfers between devices with their start and end apart: 2, of which 2 were waited for; matrix products, arithmetic and copies ran while one was open for 0% of the time, Pallas kernels for 0%

commit v1 on v0

v1 whole, which is shorter than its diff:
```python
import functools

import jax
import jax.numpy as jnp
from jax import lax
from jax.experimental import pallas as pl
from jax.experimental.pallas import tpu as pltpu
from jax.sharding import PartitionSpec as P

ridge = 0.1
epsilon = 1e-06
MESH = pl.DeviceIdType.MESH
HIGHEST = lax.Precision.HIGHEST
NT = (((1,), (1,)), ((), ()))
RANK = 128
PARTS = 4
PANEL = 16


def invert(normal, stage):
    rows = lax.broadcasted_iota(jnp.int32, (RANK, RANK), 0)
    cols = lax.broadcasted_iota(jnp.int32, (RANK, RANK), 1)
    panel_row = lax.broadcasted_iota(jnp.int32, (PANEL, RANK), 0)
    panel_col = lax.broadcasted_iota(jnp.int32, (PANEL, RANK), 1)
    a = normal
    for first in range(0, RANK, PANEL):
        panel = a[first : first + PANEL, :]
        columns = [
            jnp.broadcast_to(panel[:, first + j : first + j + 1], (PANEL, RANK))
            for j in range(PANEL)
        ]
        inside = (panel_col >= first) & (panel_col < first + PANEL)
        unit = jnp.where(panel_col - first == panel_row, 1.0, 0.0)
        right = jnp.where(inside, unit, panel)
        for k in range(PANEL):
            pivot = columns[k]
            scale = 1.0 / pivot[k : k + 1, :]
            is_pivot = panel_row == k
            top = right[k : k + 1, :] * scale
            right = jnp.where(is_pivot, top, right - pivot * top)
            for j in range(k + 1, PANEL):
                top = columns[j][k : k + 1, :] * scale
                columns[j] = jnp.where(is_pivot, top, columns[j] - pivot * top)
        parts = [right]
        if first:
            parts = [jnp.zeros((first, RANK), jnp.float32)] + parts
        if first + PANEL < RANK:
            parts = parts + [jnp.zeros((RANK - first - PANEL, RANK), jnp.float32)]
        spread = jnp.concatenate(parts, axis=0)
        in_cols = (cols >= first) & (cols < first + PANEL)
        in_rows = (rows >= first) & (rows < first + PANEL)
        update = jnp.dot(
            jnp.where(in_cols, a, 0.0), spread, precision=HIGHEST, preferred_element_type=jnp.float32
        )
        a = jnp.where(in_rows, spread, jnp.where(in_cols, 0.0, a) - update)
    return a


def gram(factor_ref, pad_ref):
    pad_ref[...] = jnp.zeros_like(pad_ref)
    pad_ref[0 : factor_ref.shape[0], :] = factor_ref[...]
    full = pad_ref[...]
    return jnp.dot(full.T, full, precision=HIGHEST, preferred_element_type=jnp.float32)


def main_kernel(
    grid_sizes, yields, model, scen, year, raw, g_out,
    ybuf, mbuf, sbuf, yearbuf, khat, kht, pad, csend, crecv, ysend, yrecv, own,
    gd, gcr, gy, gz, gx, gfin,
    yield_sems, factor_sems, send_sems, recv_sems,
):
    nz, nx = grid_sizes
    s = lax.axis_index("scen")
    c = lax.axis_index("cell")
    core = s % 2
    ylo = s // 2
    yhi = c % 2
    y = yhi * 2 + ylo
    x = (c // 2) % nx
    z = c // (2 * nx)
    quarter = yields.shape[1] // PARTS
    steps = csend.shape[0] // 2
    width = quarter // steps

    def device(core, y, z, x):
        return ((y % 2) * 2 + core, (z * nx + x) * 2 + y // 2)

    partner = device(1 - core, y, z, x)
    across = ((1 - ylo) * 2 + core, c)
    diagonal = ((1 - ylo) * 2 + 1 - core, c)
    y_peers = [device(core, (y + k) % 4, z, x) for k in (1, 2, 3)]
    z_peers = [device(core, y, (z + k) % nz, x) for k in range(1, nz)]
    x_peers = [device(core, y, z, (x + k) % nx) for k in range(1, nx)]

    counter = [0]
    sent = []

    def send(src, dst, target):
        n = counter[0]
        counter[0] += 1
        copy = pltpu.make_async_remote_copy(
            src_ref=src, dst_ref=dst, send_sem=send_sems.at[n], recv_sem=recv_sems.at[n],
            device_id=target, device_id_type=MESH,
        )
        copy.start()
        sent.append(copy)
        return copy

    q_across = (1 - ylo) * 2 + core
    q_diagonal = (1 - ylo) * 2 + 1 - core
    q_partner = ylo * 2 + 1 - core
    order = []
    for first, second in ((q_diagonal, q_across), (q_partner, s)):
        for j in range(steps):
            order += [(first, j), (second, j)]

    factor_copies = [
        pltpu.make_async_copy(src, dst, factor_sems.at[i])
        for i, (src, dst) in enumerate(((model, mbuf), (scen, sbuf.at[s]), (year, yearbuf)))
    ]
    for copy in factor_copies:
        copy.start()
    loads = []
    for i, (q, j) in enumerate(order):
        start = pl.multiple_of(q * quarter + j * width, width)
        loads.append(
            pltpu.make_async_copy(yields.at[:, pl.ds(start, width)], ybuf.at[i], yield_sems.at[i])
        )
    ahead = 4
    for copy in loads[:ahead]:
        copy.start()

    barrier = pltpu.get_barrier_semaphore()
    peers = [partner, diagonal] + y_peers + z_peers + x_peers
    for peer in peers:
        pl.semaphore_signal(barrier, inc=1, device_id=peer, device_id_type=MESH)

    for copy in factor_copies:
        copy.wait()
    local_scen = sbuf[s]
    years = yearbuf.shape[0]
    block = 8 * years
    for m in range(mbuf.shape[0]):
        ms = mbuf[m : m + 1, :] * local_scen
        khat[m * block : (m + 1) * block, :] = (ms[None, :, :] * yearbuf[...][:, None, :]).reshape(
            block, RANK
        )
    depth = khat.shape[0]
    for first in range(0, depth, RANK):
        size = min(RANK, depth - first)
        kht[:, first : first + size] = khat[first : first + size, :].T.astype(jnp.bfloat16)

    def product(i):
        loads[i].wait()
        if i + ahead < len(loads):
            loads[i + ahead].start()
        return jnp.dot(kht[...], ybuf[i], preferred_element_type=jnp.float32)

    csend[0] = product(0)
    pl.semaphore_wait(barrier, len(peers))
    scen_copies = [send(sbuf.at[s], sbuf.at[s], peer) for peer in (partner, across, diagonal)]
    to_partner = [send(csend.at[0], crecv.at[0], partner)]
    crossings = []
    for j in range(steps):
        ysend[j] = product(2 * j + 1)
        n = j + 1
        csend[n] = product(2 * n)
        to_partner.append(send(csend.at[n], crecv.at[n], partner))
        to_partner[j].wait_recv()
        ysend[j] = ysend[j] + crecv[j]
        crossings.append(send(ysend.at[j], yrecv.at[j], across))
    for j in range(steps):
        n = steps + j
        own[j] = product(2 * n + 1)
        if j + 1 < steps:
            csend[n + 1] = product(2 * n + 2)
            to_partner.append(send(csend.at[n + 1], crecv.at[n + 1], partner))

    for copy in scen_copies:
        copy.wait_recv()
    gram_model = gram(mbuf, pad)
    gram_year = gram(yearbuf, pad)
    whole_scen = sbuf[...].reshape(PARTS * sbuf.shape[1], RANK)
    pad[...] = jnp.zeros_like(pad)
    pad[0 : PARTS * sbuf.shape[1], :] = whole_scen
    full = pad[...]
    gram_scen = jnp.dot(full.T, full, precision=HIGHEST, preferred_element_type=jnp.float32)
    rows = lax.broadcasted_iota(jnp.int32, (RANK, RANK), 0)
    cols = lax.broadcasted_iota(jnp.int32, (RANK, RANK), 1)
    normal = gram_model * gram_scen * gram_year + jnp.where(rows == cols, ridge, 0.0)
    inverse = invert(normal, pad)

    def rows_of(q, j):
        return pl.ds(pl.multiple_of(q * quarter + j * width, width), width)

    gathers, late = [], []
    total = jnp.zeros((RANK, RANK), jnp.float32)
    for j in range(steps):
        to_partner[steps + j].wait_recv()
        crossings[j].wait_recv()
        summed = own[j] + crecv[steps + j] + yrecv[j]
        solved = jnp.dot(inverse, summed, precision=HIGHEST, preferred_element_type=jnp.float32)
        raw[rows_of(s, j), :] = solved.T
        here = raw.at[rows_of(s, j)]
        gathers.append(send(here, here, across))
        late.append(send(here, here, partner))
        total = total + lax.dot_general(
            solved, solved, NT, precision=HIGHEST, preferred_element_type=jnp.float32
        )

    half = RANK // 2
    gd[0] = total[0:half, :]
    gd[1] = total[half:RANK, :]
    copy = send(gd.at[1 - core], gcr, partner)
    copy.wait_recv()
    value = gd[core] + gcr[...]
    for where, slots, targets in ((y, gy, y_peers), (z, gz, z_peers), (x, gx, x_peers)):
        slots[where] = value
        copies = [send(slots.at[where], slots.at[where], target) for target in targets]
        for copy in copies:
            copy.wait_recv()
        value = slots[0]
        for k in range(1, slots.shape[0]):
            value = value + slots[k]
    gfin[core] = value
    last = send(gfin.at[core], gfin.at[core], partner)

    for j in range(steps):
        gathers[j].wait_recv()
        here = raw.at[rows_of(q_across, j)]
        late.append(send(here, here, partner))
    last.wait_recv()
    g_out[...] = gfin[...].reshape(RANK, RANK)
    for copy in sent:
        copy.wait_send()
    for copy in late:
        copy.wait_recv()


def finish_kernel(cells, raw, g, factor, scale, cell_gram):
    rows = lax.broadcasted_iota(jnp.int32, (RANK, RANK), 0)
    cols = lax.broadcasted_iota(jnp.int32, (RANK, RANK), 1)
    products = g[...]
    diagonal = jnp.where(rows == cols, products, 0.0)
    along = jnp.sqrt(jnp.sum(diagonal, axis=0, keepdims=True) / cells + epsilon)
    down = jnp.sqrt(jnp.sum(diagonal, axis=1, keepdims=True) / cells + epsilon)
    scale[...] = along
    inverse = 1.0 / along
    cell_gram[...] = products * inverse * (1.0 / down) / cells
    factor[...] = raw[...] * inverse


def on_device(grid_sizes, yields, model_factor, scen_factor, year_factor):
    models, scens, years, local_cells = yields.shape
    rank = model_factor.shape[1]
    total_cells = local_cells * lax.axis_size("cell")
    flat = yields.transpose(0, 2, 1, 3).reshape(-1, local_cells)
    depth = flat.shape[0]
    quarter = local_cells // PARTS
    width = 256
    steps = quarter // width
    f32 = jnp.float32
    any_space = pl.BlockSpec(memory_space=pl.ANY)
    vmem = pl.BlockSpec(memory_space=pltpu.VMEM)
    copies = 80
    raw, products = pl.pallas_call(
        functools.partial(main_kernel, grid_sizes),
        out_shape=(
            jax.ShapeDtypeStruct((local_cells, rank), f32),
            jax.ShapeDtypeStruct((rank, rank), f32),
        ),
        in_specs=[any_space] * 4,
        out_specs=(vmem, vmem),
        scratch_shapes=[
            pltpu.VMEM((4 * steps, depth, width), jnp.bfloat16),
            pltpu.VMEM((models, rank), f32),
            pltpu.VMEM((PARTS, scens, rank), f32),
            pltpu.VMEM((years, rank), f32),
            pltpu.VMEM((depth, rank), f32),
            pltpu.VMEM((rank, depth), jnp.bfloat16),
            pltpu.VMEM((rank, rank), f32),
            pltpu.VMEM((2 * steps, rank, width), f32),
            pltpu.VMEM((2 * steps, rank, width), f32),
            pltpu.VMEM((steps, rank, width), f32),
            pltpu.VMEM((steps, rank, width), f32),
            pltpu.VMEM((steps, rank, width), f32),
            pltpu.VMEM((2, rank // 2, rank), f32),
            pltpu.VMEM((rank // 2, rank), f32),
            pltpu.VMEM((4, rank // 2, rank), f32),
            pltpu.VMEM((grid_sizes[0], rank // 2, rank), f32),
            pltpu.VMEM((grid_sizes[1], rank // 2, rank), f32),
            pltpu.VMEM((2, rank // 2, rank), f32),
            pltpu.SemaphoreType.DMA((4 * steps,)),
            pltpu.SemaphoreType.DMA((3,)),
            pltpu.SemaphoreType.DMA((copies,)),
            pltpu.SemaphoreType.DMA((copies,)),
        ],
        compiler_params=pltpu.CompilerParams(
            collective_id=0, has_side_effects=True, vmem_limit_bytes=52 << 20
        ),
    )(flat, model_factor, scen_factor, year_factor)
    cell_factor, column_scale, cell_gram = pl.pallas_call(
        functools.partial(finish_kernel, float(total_cells)),
        out_shape=(
            jax.ShapeDtypeStruct((local_cells, rank), f32),
            jax.ShapeDtypeStruct((1, rank), f32),
            jax.ShapeDtypeStruct((rank, rank), f32),
        ),
        in_specs=[vmem, vmem],
        out_specs=(vmem, vmem, vmem),
    )(raw, products)
    return cell_factor, column_scale.reshape(rank), cell_gram


def solution(mesh):
    cells = mesh.shape["cell"]
    grid_sizes = (4, cells // 8)
    in_specs = (P(None, "scen", None, "cell"), P(), P("scen", None), P())
    out_specs = (P("cell", None), P(), P())
    return jax.shard_map(
        functools.partial(on_device, grid_sizes), mesh=mesh, in_specs=in_specs, out_specs=out_specs, check_vma=False
    )
```

time: 552 us -> 55.9 us (0.10)
  the two profiles are of different devices: /device:TPU:0 before, /device:TPU:1 now
where the time goes in v1:
time: 55.9 us; the launch traced here: 55.7 us
  Pallas kernels  52.3 us (94%)
  local copies, waits for them, and re-layouts  2.7 us (5%)
  between operations  0.66 us (1%)
    pallas_call x1, Pallas kernels, on_device(): pl.pallas_call(functools.partial(main_kernel, grid_sizes), out_shape=(jax...  49.2 us
    pallas_call x1, Pallas kernels, on_device(): pl.pallas_call(functools.partial(finish_kernel, float(total_cells)), out_...  3.14 us
    unnamed x8, local copies, waits for them, and re-layouts  2.7 us

profile of v1, /device:TPU:1, one launch (start us, length us, event | category | flops | bytes accessed | tf_op | source)
XLA Modules:
  0.0 55.7 jit_solution(544850423472988467)
XLA Ops:
  0.6 0.0 copy-start.1
  0.6 0.7 %copy-done.1 = f32[30,128]{1,0:T(8,128)S(1)} copy-done((f32[30,128]{1,0:T(8,128)S(1)}, f32[30,128]{1,0:T(8,128)}, u32[]{:S(2)}) %copy-start.1) | copy-done | bytes 15384
  1.3 0.0 copy-start.2
  1.4 0.7 %copy-done.2 = f32[12,128]{1,0:T(8,128)S(1)} copy-done((f32[12,128]{1,0:T(8,128)S(1)}, f32[12,128]{1,0:T(8,128)}, u32[]{:S(2)}) %copy-start.2) | copy-done | bytes 6168
  2.0 0.0 copy-start.3
  2.0 0.7 %copy-done.3 = f32[8,128]{1,0:T(8,128)S(1)} copy-done((f32[8,128]{1,0:T(8,128)S(1)}, f32[8,128]{1,0:T(8,128)}, u32[]{:S(2)}) %copy-start.3) | copy-done | bytes 4120
  2.7 49.2 %shard_map.67 = (f32[4096,128]{1,0:T(8,128)}, f32[128,128]{1,0:T(8,128)S(1)}) custom-call(bf16[2880,4096]{1,0:T(8,128)(2,1)} %bitcast.4, f32[12,128]{1,0:T(8,128)S(1)} %copy-done.2, f32[8,128]{1,0:T(8,128)S(1)} %copy-done.3, f32[30,128]{1,0:T(8,128)S(1)} %copy-done.1), custom_call_target="tpu_custom_call" | custom-call | tf_op jit(solution)/shard_map/pallas_call | solution.py:266
  51.9 0.0 copy-start
  51.9 0.6 %copy-done = f32[128,128]{1,0:T(8,128)} copy-done((f32[128,128]{1,0:T(8,128)}, f32[128,128]{1,0:T(8,128)S(1)}, u32[]{:S(2)}) %copy-start) | copy-done | bytes 65560
  52.5 3.1 %shard_map.68 = (f32[4096,128]{1,0:T(8,128)}, f32[1,128]{1,0:T(1,128)}, f32[128,128]{1,0:T(8,128)}) custom-call(f32[4096,128]{1,0:T(8,128)} %get-tuple-element.8.raw, f32[128,128]{1,0:T(8,128)} %copy-done), custom_call_target="tpu_custom_call" | custom-call | tf_op jit(solution)/shard_map/pallas_call | solution.py:302
Async XLA Ops:
  0.6 0.7 %copy-start.1 = (f32[30,128]{1,0:T(8,128)S(1)}, f32[30,128]{1,0:T(8,128)}, u32[]{:S(2)}) copy-start(f32[30,128]{1,0:T(8,128)} %year.1) | copy-start | bytes 46084
  1.3 0.7 %copy-start.2 = (f32[12,128]{1,0:T(8,128)S(1)}, f32[12,128]{1,0:T(8,128)}, u32[]{:S(2)}) copy-start(f32[12,128]{1,0:T(8,128)} %model.1) | copy-start | bytes 18436
  2.0 0.7 %copy-start.3 = (f32[8,128]{1,0:T(8,128)S(1)}, f32[8,128]{1,0:T(8,128)}, u32[]{:S(2)}) copy-start(f32[8,128]{1,0:T(8,128)} %scen.1) | copy-start | bytes 12292
  51.9 0.6 %copy-start = (f32[128,128]{1,0:T(8,128)}, f32[128,128]{1,0:T(8,128)S(1)}, u32[]{:S(2)}) copy-start(f32[128,128]{1,0:T(8,128)S(1)} %get-tuple-element.9.g) | copy-start | bytes 196612

commit v2 on v1

--- a/solution.py
+++ b/solution.py
@@ -15,6 +15,7 @@
 RANK = 128
 PARTS = 4
 PANEL = 16
+WIDTHS = (128, 256, 256, 256, 128)
 
 
 def invert(normal, stage):
@@ -64,8 +65,8 @@
 
 
 def main_kernel(
-    grid_sizes, yields, model, scen, year, raw, g_out,
-    ybuf, mbuf, sbuf, yearbuf, khat, kht, pad, csend, crecv, ysend, yrecv, own,
+    grid_sizes, widths, yields, model, scen, year, raw, g_out,
+    ybufs, mbuf, sbuf, yearbuf, khat, kht, pad, csend, crecv, ysend, yrecv, own,
     gd, gcr, gy, gz, gx, gfin,
     yield_sems, factor_sems, send_sems, recv_sems,
 ):
@@ -79,8 +80,8 @@
     x = (c // 2) % nx
     z = c // (2 * nx)
     quarter = yields.shape[1] // PARTS
-    steps = csend.shape[0] // 2
-    width = quarter // steps
+    steps = len(widths)
+    offsets = [sum(widths[:j]) for j in range(steps)]
 
     def device(core, y, z, x):
         return ((y % 2) * 2 + core, (z * nx + x) * 2 + y // 2)
@@ -88,23 +89,40 @@
     partner = device(1 - core, y, z, x)
     across = ((1 - ylo) * 2 + core, c)
     diagonal = ((1 - ylo) * 2 + 1 - core, c)
-    y_peers = [device(core, (y + k) % 4, z, x) for k in (1, 2, 3)]
-    z_peers = [device(core, y, (z + k) % nz, x) for k in range(1, nz)]
-    x_peers = [device(core, y, z, (x + k) % nx) for k in range(1, nx)]
-
-    counter = [0]
+    y_peers = [device(core, (y + k) % 4, z, x) for k in (2, 1, 3)]
+    z_peers = [device(core, y, (z + k) % nz, x) for k in (2, 1, 3)]
+    x_peers = [device(core, y, z, (x + k) % nx) for k in (2, 1, 3)]
+    first_slot = z * (1 - core) + x * core
+    second_slot = x * (1 - core) + z * core
+    first_peers = [
+        device(core, y, (z + k * (1 - core)) % nz, (x + k * core) % nx) for k in (2, 1, 3)
+    ]
+    second_peers = [
+        device(core, y, (z + k * core) % nz, (x + k * (1 - core)) % nx) for k in (2, 1, 3)
+    ]
+
     sent = []
+    received = set()
 
     def send(src, dst, target):
-        n = counter[0]
-        counter[0] += 1
+        n = len(sent)
         copy = pltpu.make_async_remote_copy(
             src_ref=src, dst_ref=dst, send_sem=send_sems.at[n], recv_sem=recv_sems.at[n],
             device_id=target, device_id_type=MESH,
         )
         copy.start()
         sent.append(copy)
-        return copy
+        return n
+
+    left = set()
+
+    def leave(n):
+        left.add(n)
+        sent[n].wait_send()
+
+    def arrive(n):
+        received.add(n)
+        sent[n].wait_recv()
 
     q_across = (1 - ylo) * 2 + core
     q_diagonal = (1 - ylo) * 2 + 1 - core
@@ -120,16 +138,22 @@
     ]
     for copy in factor_copies:
         copy.start()
+
+    def columns(q, j):
+        return pl.ds(pl.multiple_of(q * quarter + offsets[j], 128), widths[j])
+
     loads = []
     for i, (q, j) in enumerate(order):
-        start = pl.multiple_of(q * quarter + j * width, width)
-        loads.append(
-            pltpu.make_async_copy(yields.at[:, pl.ds(start, width)], ybuf.at[i], yield_sems.at[i])
-        )
-    ahead = 4
-    for copy in loads[:ahead]:
-        copy.start()
-
+        slot = ybufs.at[i, :, pl.ds(0, widths[j])]
+        loads.append(pltpu.make_async_copy(yields.at[:, columns(q, j)], slot, yield_sems.at[i]))
+    ahead = [0]
+
+    def load_until(n):
+        for copy in loads[ahead[0] : n]:
+            copy.start()
+        ahead[0] = max(ahead[0], min(n, len(loads)))
+
+    load_until(3)
     barrier = pltpu.get_barrier_semaphore()
     peers = [partner, diagonal] + y_peers + z_peers + x_peers
     for peer in peers:
@@ -152,32 +176,46 @@
 
     def product(i):
         loads[i].wait()
-        if i + ahead < len(loads):
-            loads[i + ahead].start()
-        return jnp.dot(kht[...], ybuf[i], preferred_element_type=jnp.float32)
-
-    csend[0] = product(0)
+        load_until(i + 6)
+        return jnp.dot(
+            kht[...], ybufs[i, :, 0 : widths[order[i][1]]], preferred_element_type=jnp.float32
+        )
+
+    def part(ref, n):
+        return ref.at[n, :, pl.ds(0, widths[n % steps])]
+
+    part(csend, 0)[...] = product(0)
     pl.semaphore_wait(barrier, len(peers))
-    scen_copies = [send(sbuf.at[s], sbuf.at[s], peer) for peer in (partner, across, diagonal)]
-    to_partner = [send(csend.at[0], crecv.at[0], partner)]
+    to_partner = [send(part(csend, 0), part(crecv, 0), partner)]
+    scen_copies = []
     crossings = []
+    gathers = []
+    late = []
+
+    def rows_of(q, j):
+        return pl.ds(pl.multiple_of(q * quarter + offsets[j], 128), widths[j])
+
     for j in range(steps):
-        ysend[j] = product(2 * j + 1)
+        part(ysend, j)[...] = product(2 * j + 1)
         n = j + 1
-        csend[n] = product(2 * n)
-        to_partner.append(send(csend.at[n], crecv.at[n], partner))
-        to_partner[j].wait_recv()
-        ysend[j] = ysend[j] + crecv[j]
-        crossings.append(send(ysend.at[j], yrecv.at[j], across))
+        part(csend, n)[...] = product(2 * n)
+        to_partner.append(send(part(csend, n), part(crecv, n), partner))
+        arrive(to_partner[j])
+        part(ysend, j)[...] = part(ysend, j)[...] + part(crecv, j)[...]
+        crossings.append(send(part(ysend, j), part(yrecv, j), across))
+        if j == 0:
+            scen_copies = [
+                send(sbuf.at[s], sbuf.at[s], peer) for peer in (across, diagonal, partner)
+            ]
     for j in range(steps):
         n = steps + j
-        own[j] = product(2 * n + 1)
+        part(own, j)[...] = product(2 * n + 1)
         if j + 1 < steps:
-            csend[n + 1] = product(2 * n + 2)
-            to_partner.append(send(csend.at[n + 1], crecv.at[n + 1], partner))
-
-    for copy in scen_copies:
-        copy.wait_recv()
+            part(csend, n + 1)[...] = product(2 * n + 2)
+            to_partner.append(send(part(csend, n + 1), part(crecv, n + 1), partner))
+
+    for n in scen_copies:
+        arrive(n)
     gram_model = gram(mbuf, pad)
     gram_year = gram(yearbuf, pad)
     whole_scen = sbuf[...].reshape(PARTS * sbuf.shape[1], RANK)
@@ -190,64 +228,88 @@
     normal = gram_model * gram_scen * gram_year + jnp.where(rows == cols, ridge, 0.0)
     inverse = invert(normal, pad)
 
-    def rows_of(q, j):
-        return pl.ds(pl.multiple_of(q * quarter + j * width, width), width)
-
-    gathers, late = [], []
     total = jnp.zeros((RANK, RANK), jnp.float32)
-    for j in range(steps):
-        to_partner[steps + j].wait_recv()
-        crossings[j].wait_recv()
-        summed = own[j] + crecv[steps + j] + yrecv[j]
-        solved = jnp.dot(inverse, summed, precision=HIGHEST, preferred_element_type=jnp.float32)
+
+    def keep(j, solved):
         raw[rows_of(s, j), :] = solved.T
         here = raw.at[rows_of(s, j)]
         gathers.append(send(here, here, across))
         late.append(send(here, here, partner))
+
+    for j in range(steps):
+        arrive(to_partner[steps + j])
+        arrive(crossings[j])
+        summed = part(own, j)[...] + part(crecv, steps + j)[...] + part(yrecv, j)[...]
+        solved = jnp.dot(inverse, summed, precision=HIGHEST, preferred_element_type=jnp.float32)
         total = total + lax.dot_general(
             solved, solved, NT, precision=HIGHEST, preferred_element_type=jnp.float32
         )
+        if j + 1 < steps:
+            keep(j, solved)
 
     half = RANK // 2
     gd[0] = total[0:half, :]
     gd[1] = total[half:RANK, :]
-    copy = send(gd.at[1 - core], gcr, partner)
-    copy.wait_recv()
+    halves = send(gd.at[1 - core], gcr, partner)
+    keep(steps - 1, solved)
+    arrive(halves)
     value = gd[core] + gcr[...]
-    for where, slots, targets in ((y, gy, y_peers), (z, gz, z_peers), (x, gx, x_peers)):
+    for phase, (where, slots, targets) in enumerate(
+        ((first_slot, gz, first_peers), (second_slot, gx, second_peers), (y, gy, y_peers))
+    ):
         slots[where] = value
+        done = list(sent)
         copies = [send(slots.at[where], slots.at[where], target) for target in targets]
-        for copy in copies:
-            copy.wait_recv()
+        if phase == 2:
+            for j in range(steps):
+                arrive(gathers[j])
+                here = raw.at[rows_of(q_across, j)]
+                late.append(send(here, here, partner))
+        for n, copy in enumerate(done):
+            if n not in left and (phase == 2 or n not in gathers):
+                leave(n)
+        for n in copies:
+            arrive(n)
         value = slots[0]
         for k in range(1, slots.shape[0]):
             value = value + slots[k]
     gfin[core] = value
     last = send(gfin.at[core], gfin.at[core], partner)
-
-    for j in range(steps):
-        gathers[j].wait_recv()
-        here = raw.at[rows_of(q_across, j)]
-        late.append(send(here, here, partner))
-    last.wait_recv()
+    for n in range(len(sent)):
+        if n != last:
+            if n not in left:
+                leave(n)
+            if n not in received:
+                arrive(n)
+    arrive(last)
     g_out[...] = gfin[...].reshape(RANK, RANK)
-    for copy in sent:
-        copy.wait_send()
-    for copy in late:
-        copy.wait_recv()
-
-
-def finish_kernel(cells, raw, g, factor, scale, cell_gram):
+    leave(last)
+
+
+def finish_kernel(cells, raw, g, factor, scale, cell_gram, scaled, small, grams, sems):
     rows = lax.broadcasted_iota(jnp.int32, (RANK, RANK), 0)
     cols = lax.broadcasted_iota(jnp.int32, (RANK, RANK), 1)
     products = g[...]
     diagonal = jnp.where(rows == cols, products, 0.0)
     along = jnp.sqrt(jnp.sum(diagonal, axis=0, keepdims=True) / cells + epsilon)
+    inverse = 1.0 / along
+    copies = []
+    count = sems.shape[0] - 2
+    rows_each = raw.shape[0] // count
+    for i in range(count):
+        here = pl.ds(i * rows_each, rows_each)
+        scaled[here, :] = raw[here, :] * inverse
+        copies.append(pltpu.make_async_copy(scaled.at[here], factor.at[here], sems.at[i]))
+        copies[-1].start()
     down = jnp.sqrt(jnp.sum(diagonal, axis=1, keepdims=True) / cells + epsilon)
-    scale[...] = along
-    inverse = 1.0 / along
-    cell_gram[...] = products * inverse * (1.0 / down) / cells
-    factor[...] = raw[...] * inverse
+    small[...] = along
+    grams[...] = products * inverse * (1.0 / down) / cells
+    copies.append(pltpu.make_async_copy(small, scale, sems.at[count]))
+    copies.append(pltpu.make_async_copy(grams, cell_gram, sems.at[count + 1]))
+    copies[-1].start()
+    copies[-2].start()
+    for copy in copies:
+        copy.wait()
 
 
 def on_device(grid_sizes, yields, model_factor, scen_factor, year_factor):
@@ -256,20 +318,23 @@
     total_cells = local_cells * lax.axis_size("cell")
     flat = yields.transpose(0, 2, 1, 3).reshape(-1, local_cells)
     depth = flat.shape[0]
-    quarter = local_cells // PARTS
-    width = 256
-    steps = quarter // width
+    steps = len(WIDTHS)
+    width = max(WIDTHS)
     f32 = jnp.float32
-    any_space = pl.BlockSpec(memory_space=pl.ANY)
+    hbm = pl.BlockSpec(memory_space=pltpu.HBM)
     vmem = pl.BlockSpec(memory_space=pltpu.VMEM)
-    copies = 80
+    copies = 64
+    operands = [
+        pltpu.with_memory_space_constraint(array, pltpu.HBM)
+        for array in (flat, model_factor, scen_factor, year_factor)
+    ]
     raw, products = pl.pallas_call(
-        functools.partial(main_kernel, grid_sizes),
+        functools.partial(main_kernel, grid_sizes, WIDTHS),
         out_shape=(
-            jax.ShapeDtypeStruct((local_cells, rank), f32),
-            jax.ShapeDtypeStruct((rank, rank), f32),
+            pltpu.VMEM((local_cells, rank), f32),
+            pltpu.VMEM((rank, rank), f32),
         ),
-        in_specs=[any_space] * 4,
+        in_specs=[hbm] * 4,
         out_specs=(vmem, vmem),
         scratch_shapes=[
             pltpu.VMEM((4 * steps, depth, width), jnp.bfloat16),
@@ -296,9 +361,9 @@
             pltpu.SemaphoreType.DMA((copies,)),
         ],
         compiler_params=pltpu.CompilerParams(
-            collective_id=0, has_side_effects=True, vmem_limit_bytes=52 << 20
+            collective_id=0, has_side_effects=True, vmem_limit_bytes=48 << 20
         ),
-    )(flat, model_factor, scen_factor, year_factor)
+    )(*operands)
     cell_factor, column_scale, cell_gram = pl.pallas_call(
         functools.partial(finish_kernel, float(total_cells)),
         out_shape=(
@@ -307,7 +372,14 @@
             jax.ShapeDtypeStruct((rank, rank), f32),
         ),
         in_specs=[vmem, vmem],
-        out_specs=(vmem, vmem, vmem),
+        out_specs=(hbm, hbm, hbm),
+        scratch_shapes=[
+            pltpu.VMEM((local_cells, rank), f32),
+            pltpu.VMEM((1, rank), f32),
+            pltpu.VMEM((rank, rank), f32),
+            pltpu.SemaphoreType.DMA((10,)),
+        ],
+        compiler_params=pltpu.CompilerParams(vmem_limit_bytes=16 << 20),
     )(raw, products)
     return cell_factor, column_scale.reshape(rank), cell_gram
 

time: 55.9 us -> 42.4 us (0.76)
  Pallas kernels: 52.3 us -> 41.6 us
  local copies, waits for them, and re-layouts: 2.7 us -> 0 us
    pallas_call x1, Pallas kernels: 49.2 us -> 40.1 us  [on_device(): pl.pallas_call(functools.partial(main_kernel, grid_sizes, WIDTHS), out_sh...]
    unnamed x8 -> x0, local copies, waits for them, and re-layouts: 2.7 us -> none
    pallas_call x1, Pallas kernels: 3.14 us -> 1.47 us  [on_device(): pl.pallas_call(functools.partial(finish_kernel, float(total_cells)), out_...]
where the time goes in v2:
time: 42.4 us; the launch traced here: 42.2 us
  Pallas kernels  41.6 us (98%)
  between operations  0.64 us (2%)
    pallas_call x1, Pallas kernels, on_device(): pl.pallas_call(functools.partial(main_kernel, grid_sizes, WIDTHS), out_sh...  40.1 us
    pallas_call x1, Pallas kernels, on_device(): pl.pallas_call(functools.partial(finish_kernel, float(total_cells)), out_...  1.47 us

profile of v2, /device:TPU:1, one launch (start us, length us, event | category | flops | bytes accessed | tf_op | source)
XLA Modules:
  0.0 42.2 jit_solution(14699185170732376856)
XLA Ops:
  0.6 40.1 %shard_map.67 = (f32[4096,128]{1,0:T(8,128)S(1)}, f32[128,128]{1,0:T(8,128)S(1)}) custom-call(bf16[2880,4096]{1,0:T(8,128)(2,1)} %bitcast.4, f32[12,128]{1,0:T(8,128)} %model.1, f32[8,128]{1,0:T(8,128)} %scen.1, f32[30,128]{1,0:T(8,128)} %year.1), custom_call_target="tpu_custom_call" | custom-call | tf_op jit(solution)/shard_map/pallas_call | solution.py:331
  40.7 1.5 %shard_map.68 = (f32[4096,128]{1,0:T(8,128)}, f32[1,128]{1,0:T(1,128)}, f32[128,128]{1,0:T(8,128)}) custom-call(f32[4096,128]{1,0:T(8,128)S(1)} %get-tuple-element.8.raw, f32[128,128]{1,0:T(8,128)S(1)} %get-tuple-element.9.g), custom_call_target="tpu_custom_call" | custom-call | tf_op jit(solution)/shard_map/pallas_call | solution.py:367

commit v3 on v2

--- a/solution.py
+++ b/solution.py
@@ -15,7 +15,7 @@
 RANK = 128
 PARTS = 4
 PANEL = 16
-WIDTHS = (128, 256, 256, 256, 128)
+WIDTHS = (128, 384, 384, 128)
 
 
 def invert(normal, stage):
@@ -153,7 +153,7 @@
             copy.start()
         ahead[0] = max(ahead[0], min(n, len(loads)))
 
-    load_until(3)
+    load_until(2)
     barrier = pltpu.get_barrier_semaphore()
     peers = [partner, diagonal] + y_peers + z_peers + x_peers
     for peer in peers:
@@ -198,8 +198,9 @@
     for j in range(steps):
         part(ysend, j)[...] = product(2 * j + 1)
         n = j + 1
-        part(csend, n)[...] = product(2 * n)
-        to_partner.append(send(part(csend, n), part(crecv, n), partner))
+        if j:
+            part(csend, n)[...] = product(2 * n)
+            to_partner.append(send(part(csend, n), part(crecv, n), partner))
         arrive(to_partner[j])
         part(ysend, j)[...] = part(ysend, j)[...] + part(crecv, j)[...]
         crossings.append(send(part(ysend, j), part(yrecv, j), across))
@@ -207,6 +208,8 @@
             scen_copies = [
                 send(sbuf.at[s], sbuf.at[s], peer) for peer in (across, diagonal, partner)
             ]
+            part(csend, n)[...] = product(2 * n)
+            to_partner.append(send(part(csend, n), part(crecv, n), partner))
     for j in range(steps):
         n = steps + j
         part(own, j)[...] = product(2 * n + 1)

time: 42.4 us -> 40.1 us (0.946)
  Pallas kernels: 41.6 us -> 39.3 us
    pallas_call x1, Pallas kernels: 40.1 us -> 37.8 us  [on_device(): pl.pallas_call(functools.partial(main_kernel, grid_sizes, WIDTHS), out_sh...]
where the time goes in v3:
time: 40.1 us; the launch traced here: 39.9 us
  Pallas kernels  39.3 us (98%)
  between operations  0.64 us (2%)
    pallas_call x1, Pallas kernels, on_device(): pl.pallas_call(functools.partial(main_kernel, grid_sizes, WIDTHS), out_sh...  37.8 us
    pallas_call x1, Pallas kernels, on_device(): pl.pallas_call(functools.partial(finish_kernel, float(total_cells)), out_...  1.47 us

profile of v3, /device:TPU:1, one launch (start us, length us, event | category | flops | bytes accessed | tf_op | source)
XLA Modules:
  0.0 39.9 jit_solution(13913890101055076425)
XLA Ops:
  0.6 37.8 %shard_map.67 = (f32[4096,128]{1,0:T(8,128)S(1)}, f32[128,128]{1,0:T(8,128)S(1)}) custom-call(bf16[2880,4096]{1,0:T(8,128)(2,1)} %bitcast.4, f32[12,128]{1,0:T(8,128)} %model.1, f32[8,128]{1,0:T(8,128)} %scen.1, f32[30,128]{1,0:T(8,128)} %year.1), custom_call_target="tpu_custom_call" | custom-call | tf_op jit(solution)/shard_map/pallas_call | solution.py:334
  38.5 1.5 %shard_map.68 = (f32[4096,128]{1,0:T(8,128)}, f32[1,128]{1,0:T(1,128)}, f32[128,128]{1,0:T(8,128)}) custom-call(f32[4096,128]{1,0:T(8,128)S(1)} %get-tuple-element.8.raw, f32[128,128]{1,0:T(8,128)S(1)} %get-tuple-element.9.g), custom_call_target="tpu_custom_call" | custom-call | tf_op jit(solution)/shard_map/pallas_call | solution.py:370

commit v4 on v3

--- a/solution.py
+++ b/solution.py
@@ -64,6 +64,30 @@
     return jnp.dot(full.T, full, precision=HIGHEST, preferred_element_type=jnp.float32)
 
 
+def turn(block, lanes):
+    return jnp.concatenate([block[:, RANK - lanes :], block[:, : RANK - lanes]], axis=1)
+
+
+def pack(whole, packed):
+    lane = lax.broadcasted_iota(jnp.int32, (32, RANK), 1)
+    packed[0, 0:32, :] = whole[0:32, :]
+    packed[1, 0:32, :] = jnp.where(lane < 32, turn(whole[96:128, :], 32), whole[32:64, :])
+    rest = jnp.where(lane[0:16] < 64, turn(whole[80:96, :], 64), whole[64:80, :])
+    packed[0, 32:40, :] = rest[0:8, :]
+    packed[1, 32:40, :] = rest[8:16, :]
+
+
+def unpack(packed):
+    rest = jnp.concatenate([packed[0, 32:40, :], packed[1, 32:40, :]], axis=0)
+    second = packed[1, 0:32, :]
+    upper = jnp.concatenate(
+        [packed[0, 0:32, :], second, rest, turn(rest, 64), turn(second, 96)], axis=0
+    )
+    rows = jnp.right_shift(lax.broadcasted_iota(jnp.int32, (RANK, RANK), 0), 5)
+    cols = jnp.right_shift(lax.broadcasted_iota(jnp.int32, (RANK, RANK), 1), 5)
+    return jnp.where(cols >= rows, upper, upper.T)
+
+
 def main_kernel(
     grid_sizes, widths, yields, model, scen, year, raw, g_out,
     ybufs, mbuf, sbuf, yearbuf, khat, kht, pad, csend, crecv, ysend, yrecv, own,
@@ -250,9 +274,7 @@
         if j + 1 < steps:
             keep(j, solved)
 
-    half = RANK // 2
-    gd[0] = total[0:half, :]
-    gd[1] = total[half:RANK, :]
+    pack(total, gd)
     halves = send(gd.at[1 - core], gcr, partner)
     keep(steps - 1, solved)
     arrive(halves)
@@ -285,7 +307,7 @@
             if n not in received:
                 arrive(n)
     arrive(last)
-    g_out[...] = gfin[...].reshape(RANK, RANK)
+    g_out[...] = unpack(gfin)
     leave(last)
 
 
@@ -352,12 +374,12 @@
             pltpu.VMEM((steps, rank, width), f32),
             pltpu.VMEM((steps, rank, width), f32),
             pltpu.VMEM((steps, rank, width), f32),
-            pltpu.VMEM((2, rank // 2, rank), f32),
-            pltpu.VMEM((rank // 2, rank), f32),
-            pltpu.VMEM((4, rank // 2, rank), f32),
-            pltpu.VMEM((grid_sizes[0], rank // 2, rank), f32),
-            pltpu.VMEM((grid_sizes[1], rank // 2, rank), f32),
-            pltpu.VMEM((2, rank // 2, rank), f32),
+            pltpu.VMEM((2, 40, rank), f32),
+            pltpu.VMEM((40, rank), f32),
+            pltpu.VMEM((4, 40, rank), f32),
+            pltpu.VMEM((grid_sizes[0], 40, rank), f32),
+            pltpu.VMEM((grid_sizes[1], 40, rank), f32),
+            pltpu.VMEM((2, 40, rank), f32),
             pltpu.SemaphoreType.DMA((4 * steps,)),
             pltpu.SemaphoreType.DMA((3,)),
             pltpu.SemaphoreType.DMA((copies,)),

time: 40.1 us -> 39.5 us (0.985)
  Pallas kernels: 39.3 us -> 38.7 us
    pallas_call x1, Pallas kernels: 37.8 us -> 37.3 us  [on_device(): pl.pallas_call(functools.partial(main_kernel, grid_sizes, WIDTHS), out_sh...]
where the time goes in v4:
time: 39.5 us; the launch traced here: 39.4 us
  Pallas kernels  38.7 us (98%)
  between operations  0.64 us (2%)
    pallas_call x1, Pallas kernels, on_device(): pl.pallas_call(functools.partial(main_kernel, grid_sizes, WIDTHS), out_sh...  37.3 us
    pallas_call x1, Pallas kernels, on_device(): pl.pallas_call(functools.partial(finish_kernel, float(total_cells)), out_...  1.47 us

profile of v4, /device:TPU:1, one launch (start us, length us, event | category | flops | bytes accessed | tf_op | source)
XLA Modules:
  0.0 39.4 jit_solution(10683301750738609169)
XLA Ops:
  0.6 37.3 %shard_map.67 = (f32[4096,128]{1,0:T(8,128)S(1)}, f32[128,128]{1,0:T(8,128)S(1)}) custom-call(bf16[2880,4096]{1,0:T(8,128)(2,1)} %bitcast.4, f32[12,128]{1,0:T(8,128)} %model.1, f32[8,128]{1,0:T(8,128)} %scen.1, f32[30,128]{1,0:T(8,128)} %year.1), custom_call_target="tpu_custom_call" | custom-call | tf_op jit(solution)/shard_map/pallas_call | solution.py:356
  37.9 1.5 %shard_map.68 = (f32[4096,128]{1,0:T(8,128)}, f32[1,128]{1,0:T(1,128)}, f32[128,128]{1,0:T(8,128)}) custom-call(f32[4096,128]{1,0:T(8,128)S(1)} %get-tuple-element.8.raw, f32[128,128]{1,0:T(8,128)S(1)} %get-tuple-element.9.g), custom_call_target="tpu_custom_call" | custom-call | tf_op jit(solution)/shard_map/pallas_call | solution.py:392

commit v5 on v4

--- a/solution.py
+++ b/solution.py
@@ -15,7 +15,7 @@
 RANK = 128
 PARTS = 4
 PANEL = 16
-WIDTHS = (128, 384, 384, 128)
+WIDTHS = (128, 256, 384, 256)
 
 
 def invert(normal, stage):

time: 39.5 us -> 39.7 us (level)
  no operation moved by 1% of the time
where the time goes in v5:
time: 39.7 us; the launch traced here: 39.6 us
  Pallas kernels  39 us (98%)
  between operations  0.64 us (2%)
    pallas_call x1, Pallas kernels, on_device(): pl.pallas_call(functools.partial(main_kernel, grid_sizes, WIDTHS), out_sh...  37.5 us
    pallas_call x1, Pallas kernels, on_device(): pl.pallas_call(functools.partial(finish_kernel, float(total_cells)), out_...  1.47 us

profile of v5, /device:TPU:1, one launch (start us, length us, event | category | flops | bytes accessed | tf_op | source)
XLA Modules:
  0.0 39.6 jit_solution(18005076668832176994)
XLA Ops:
  0.6 37.5 %shard_map.67 = (f32[4096,128]{1,0:T(8,128)S(1)}, f32[128,128]{1,0:T(8,128)S(1)}) custom-call(bf16[2880,4096]{1,0:T(8,128)(2,1)} %bitcast.4, f32[12,128]{1,0:T(8,128)} %model.1, f32[8,128]{1,0:T(8,128)} %scen.1, f32[30,128]{1,0:T(8,128)} %year.1), custom_call_target="tpu_custom_call" | custom-call | tf_op jit(solution)/shard_map/pallas_call | solution.py:356
  38.1 1.5 %shard_map.68 = (f32[4096,128]{1,0:T(8,128)}, f32[1,128]{1,0:T(1,128)}, f32[128,128]{1,0:T(8,128)}) custom-call(f32[4096,128]{1,0:T(8,128)S(1)} %get-tuple-element.8.raw, f32[128,128]{1,0:T(8,128)S(1)} %get-tuple-element.9.g), custom_call_target="tpu_custom_call" | custom-call | tf_op jit(solution)/shard_map/pallas_call | solution.py:392
